TPU v7x, 512 devices: a whole 4x4x16 slice. The times are simulated.
512 devices in a mesh: grp: 16 (over y, x), dev: 32 (over z, core).
Axes of the slice: x: 4, y: 4, z: 16, core: 2. Of those that a mesh axis runs over, the one named last changes fastest.
Arguments:
- particles: float32 [2048, 5, 128], P(('grp', 'dev')), as said below
- entropy: float32 [2048, 128], P(('grp', 'dev')), may hold values from 0.5 to 2
- lists: int32 [2048, 64], P(('grp', 'dev')), may hold values from 0 to 2047, as said below
- counts: int32 [2048], P(('grp', 'dev')), may hold values from 16 to 64, as said below
Outputs:
- density: float32 [2048, 128], P(('grp', 'dev'))
- accel: float32 [2048, 3, 128], P(('grp', 'dev'))
Inputs may be any that keep to these rules, and one draw needn't show every extreme that they name: lists[c, 0] = c; every id lies in the group of c or in one of the two groups next to it, counting groups of 128 cells around a loop. `counts`: each count is a multiple of 16. `particles`: coordinates in 0 to 1 within the group's slab, masses positive, smoothing lengths from 0.3 to 0.6.
All inputs are finite; a program needn't handle non-finite values.
Results may differ from a plain program's by a relative error of at most 0.0003.
Values sent between devices are 32-bit elements; how exact they have to be, the bound alone decides.
A program may use at most 64 MiB of HBM per device.

v0:
```python
import math

import jax
import jax.numpy as jnp
from jax import lax
from jax.sharding import PartitionSpec as P

NBLK = 8


norm_const = 21.0 / (16.0 * math.pi)


def padded(block, sides, width):
    for axis, dim in sides:
        count = lax.axis_size(axis)
        forward = [(i, i + 1) for i in range(count - 1)]
        forward.append((count - 1, 0))
        backward = [(target, source) for source, target in forward]
        low = lax.ppermute(
            lax.slice_in_dim(block, block.shape[dim] - width, None, axis=dim), axis, forward
        )
        high = lax.ppermute(lax.slice_in_dim(block, 0, width, axis=dim), axis, backward)
        block = jnp.concatenate([low, block, high], axis=dim)
    return block


def laid_out(blocks, dim):
    blocks = jnp.moveaxis(blocks, 0, dim)
    lengths = blocks.shape
    return blocks.reshape(*lengths[:dim], lengths[dim] * lengths[dim + 1], *lengths[dim + 2 :])


def copy_for_each(shard, axis):
    copies = jnp.broadcast_to(shard, (lax.axis_size(axis), *shard.shape))
    return lax.all_to_all(copies, axis, split_axis=0, concat_axis=0, tiled=True)


def collect(shard, axis, dim):
    return laid_out(copy_for_each(shard, axis), dim)


def kernel_parts(dist_sq, smooth):
    ratio = jnp.sqrt(dist_sq) / smooth
    base_of = jnp.maximum(1.0 - 0.5 * ratio, 0.0)
    kernel = norm_const / smooth**3 * base_of**4 * (1.0 + 2.0 * ratio)
    slope = -5.0 * norm_const / smooth**5 * base_of**3
    return (kernel, slope)


def on_device(particles, entropy, lists, counts):
    own_cells = particles.shape[0]
    groups = lax.axis_size("grp")
    members = lax.axis_size("dev")
    group_cells = own_cells * members
    group_at = lax.axis_index("grp")
    group_of = lists // group_cells
    within = lists % group_cells
    side_of = (group_of - group_at + 1 + groups) % groups
    shift_all = (side_of - 1).astype(jnp.float32)
    gathered = lax.all_gather(particles, "dev", axis=0, tiled=True)
    extended = padded(gathered, (("grp", 0),), group_cells)
    slots_ext = side_of * group_cells + within
    upper = (jnp.max(counts) + NBLK - 1) // NBLK
    slot_range = jnp.arange(NBLK, dtype=jnp.int32)
    own_smooth = particles[:, None, 4, :, None]
    unit_first = jnp.array([1.0, 0.0, 0.0], dtype=jnp.float32)

    def fetch_block(block_at):
        chosen = lax.dynamic_slice_in_dim(slots_ext, block_at * NBLK, NBLK, 1)
        shift_blk = lax.dynamic_slice_in_dim(shift_all, block_at * NBLK, NBLK, 1)
        others = extended[chosen]
        live = ((block_at * NBLK + slot_range)[None, :] < counts[:, None]).astype(jnp.float32)
        offset = particles[:, None, :3, :, None] - others[:, :, :3, None, :]
        offset = offset - shift_blk[:, :, None, None, None] * unit_first[None, None, :, None, None]
        dist_sq = jnp.sum(offset * offset, axis=2)
        return (chosen, others, live, offset, dist_sq)

    def density_step(block_at, total):
        chosen, others, live, offset, dist_sq = fetch_block(block_at)
        kernel, slope = kernel_parts(dist_sq, own_smooth)
        return total + jnp.sum(
            live[:, :, None, None] * others[:, :, 3, None, :] * kernel, axis=(1, 3)
        )

    density = lax.fori_loop(
        0, upper, density_step, jnp.zeros((own_cells, particles.shape[2]), jnp.float32)
    )
    pressure = entropy * density ** (5.0 / 3.0)
    weight = pressure / (density * density)
    weight_grp = collect(weight, "dev", 0)
    weight_ext = padded(weight_grp, (("grp", 0),), group_cells)

    def force_step(block_at, total):
        chosen, others, live, offset, dist_sq = fetch_block(block_at)
        kernel_i, slope_i = kernel_parts(dist_sq, own_smooth)
        kernel_j, slope_j = kernel_parts(dist_sq, others[:, :, 4, None, :])
        factor = (
            live[:, :, None, None]
            * others[:, :, 3, None, :]
            * (weight[:, None, :, None] * slope_i + weight_ext[chosen][:, :, None, :] * slope_j)
        )
        return total - jnp.sum(factor[:, :, None] * offset, axis=(1, 4))

    accel = lax.fori_loop(
        0, upper, force_step, jnp.zeros((own_cells, 3, particles.shape[2]), jnp.float32)
    )
    return (density, accel)


def solution(mesh):
    return jax.shard_map(
        on_device,
        mesh=mesh,
        in_specs=(
            P(("grp", "dev"), None, None),
            P(("grp", "dev"), None),
            P(("grp", "dev"), None),
            P(("grp", "dev")),
        ),
        out_specs=(P(("grp", "dev"), None), P(("grp", "dev"), None, None)),
        check_vma=False,
    )
```

profile of v0, /device:TPU:1, one launch (start us, length us, event | category | flops | bytes accessed | tf_op | source)
XLA Modules:
  0.0 174.4 jit_solution(12163319872802415283)
XLA Ops:
  0.7 0.7 copy.18
  1.4 39.0 %all_gather.3 = f32[128,5,128]{2,1,0:T(8,128)S(1)} all-gather(f32[4,5,128]{2,1,0:T(8,128)S(1)} %copy.18), channel_id=1, replica_groups=mesh['grp'=16,'dev'=32] {'dev'}, dimensions={0}, use_global_device_ids=true | all-gather | bytes 337920 | tf_op jit(solution)/shard_map/all_gather | solution.py:61
  40.3 3.1 %collective-permute-start = (f32[128,5,128]{2,1,0:T(8,128)S(1)}, f32[128,5,128]{2,1,0:T(8,128)S(1)}, u32[]{:S(2)}, u32[]{:S(2)}) collective-permute-start(f32[128,5,128]{2,1,0:T(8,128)S(1)} %all_gather.3), channel_id=1, source_target_pairs={{0,32},{32,64},{64,96},{96,128},{128,160},{160,192},{192,224},{224... | collective-permute-start | bytes 983048 | tf_op jit(solution)/shard_map/ppermute | solution.py:20
  43.5 5.6 %collective-permute-start.1 = (f32[128,5,128]{2,1,0:T(8,128)S(1)}, f32[128,5,128]{2,1,0:T(8,128)S(1)}, u32[]{:S(2)}, u32[]{:S(2)}) collective-permute-start(f32[128,5,128]{2,1,0:T(8,128)S(1)} %all_gather.3), channel_id=1, source_target_pairs={{32,0},{64,32},{96,64},{128,96},{160,128},{192,160},{224,192},{256... | collective-permute-start | bytes 983048 | tf_op jit(solution)/shard_map/ppermute | solution.py:23
  49.1 0.7 fusion.10
  49.8 0.7 add_convert_fusion
  50.5 0.7 fusion.14
  51.2 0.7 slice_bitcast_fusion
  51.9 1.3 reduce_max.9
  53.8 5.4 %collective-permute-done = f32[128,5,128]{2,1,0:T(8,128)S(1)} collective-permute-done((f32[128,5,128]{2,1,0:T(8,128)S(1)}, f32[128,5,128]{2,1,0:T(8,128)S(1)}, u32[]{:S(2)}, u32[]{:S(2)}) %collective-permute-start) | collective-permute-done | bytes 327712 | tf_op jit(solution)/shard_map/ppermute | solution.py:20
  59.3 0.8 collective-permute-done.1
  60.2 31.6 %while.28 = (s32[]{:T(128)}, f32[4,128]{1,0:T(4,128)S(1)}, s32[]{:T(128)}, s32[4]{0:T(128)S(1)}, s32[4,64]{1,0:T(4,128)S(1)}, /*index=5*/f32[384,5,128]{2,1,0:T(...) while((s32[]{:T(128)}, f32[4,128]{1,0:T(4,128)S(1)}, ...), condition=%wide.region_4.5_spmd.clone.clone, body=%wide.region_1.4_spmd.sunk.clone.clone.sunk | while | flops 12064526 | bytes 4628899 | solution.py:86
  60.4 0.6 gather_fusion
  61.2 1.3 multiply_reduce_fusion.8
  62.7 1.5 multiply_reduce_fusion.9
  64.3 0.6 gather_fusion
  65.1 1.3 multiply_reduce_fusion.8
  66.6 1.5 multiply_reduce_fusion.9
  69.1 1.3 multiply_reduce_fusion.8
  70.6 1.5 multiply_reduce_fusion.9
  73.0 1.3 multiply_reduce_fusion.8
  74.5 1.5 multiply_reduce_fusion.9
  76.2 0.6 gather_fusion
  77.0 1.3 multiply_reduce_fusion.8
  78.5 1.5 multiply_reduce_fusion.9
  80.9 1.3 multiply_reduce_fusion.8
  82.4 1.5 multiply_reduce_fusion.9
  84.9 1.3 multiply_reduce_fusion.8
  86.4 1.5 multiply_reduce_fusion.9
  88.0 0.6 gather_fusion
  88.8 1.3 multiply_reduce_fusion.8
  90.3 1.5 multiply_reduce_fusion.9
  91.9 19.8 %all_to_all.5 = f32[32,4,128]{2,1,0:T(4,128)S(1)} all-to-all(f32[32,4,128]{2,1,0:T(4,128)S(1)} %broadcast_in_dim.24), channel_id=1, replica_groups=mesh['grp'=16,'dev'=32] {'dev'}, dimensions={0} | all-to-all | bytes 131072 | tf_op jit(solution)/shard_map/all_to_all | solution.py:36
  111.6 1.9 %collective-permute-start.2 = (f32[128,128]{1,0:T(8,128)S(1)}, f32[128,128]{1,0:T(8,128)S(1)}, u32[]{:S(2)}, u32[]{:S(2)}) collective-permute-start(f32[128,128]{1,0:T(8,128)S(1)} %bitcast.62), channel_id=1, source_target_pairs={{0,32},{32,64},{64,96},{96,128},{128,160},{160,192},{192,224},{224... | collective-permute-start | bytes 196616 | tf_op jit(solution)/shard_map/ppermute | solution.py:20
  113.6 8.4 %collective-permute-start.3 = (f32[128,128]{1,0:T(8,128)S(1)}, f32[128,128]{1,0:T(8,128)S(1)}, u32[]{:S(2)}, u32[]{:S(2)}) collective-permute-start(f32[128,128]{1,0:T(8,128)S(1)} %bitcast.63), channel_id=1, source_target_pairs={{32,0},{64,32},{96,64},{128,96},{160,128},{192,160},{224,192},{256... | collective-permute-start | bytes 196616 | tf_op jit(solution)/shard_map/ppermute | solution.py:23
  122.0 1.3 collective-permute-done.3
  123.3 50.5 %while.29 = (s32[]{:T(128)}, f32[4,3,128]{2,1,0:T(4,128)S(1)}, s32[]{:T(128)}, s32[4]{0:T(128)S(1)}, s32[4,64]{1,0:T(4,128)S(1)}, /*index=5*/f32[384,5,128]{2,1,...) while((s32[]{:T(128)}, f32[4,3,128]{2,1,0:T(4,128)S(1)}, ...), condition=%wide.region_8.9_spmd.clone.clone, body=%wide.region_5.8_spmd.sunk.clone.clone.sunk | while | flops 21518092 | bytes 16909292 | solution.py:105
  124.5 1.3 multiply_reduce_fusion.10
  126.4 1.8 %fusion.20 = f32[4,8,128,128]{3,2,1,0:T(8,128)S(1)} fusion(f32[4,8,128,128]{3,2,1,0:T(8,128)S(1)} %multiply_reduce_fusion.10, f32[4,8,128]{2,1,0:T(8,128)S(1)} %bitcast.58, f32[4,8,128]{2,1,0:T(8,128)S(1)} %get-tuple-element.649, f32[4,8,128]{2,1,0:T(8,128)S(1)} %bitcast.59, f32[4,128]{1,0:T(4,128)S(1)} %bitcast.66, ...), kind=kLoop, calls=%fused_computation.24.clone.1 | loop fusion | flops 9437184 | bytes 4265984 | tf_op jit(solution)/shard_map/while/body/mul | solution.py:99
  128.2 1.4 multiply_reduce_fusion.11
  130.8 1.3 multiply_reduce_fusion.10
  132.7 1.8 %fusion.20 = f32[4,8,128,128]{3,2,1,0:T(8,128)S(1)} fusion(f32[4,8,128,128]{3,2,1,0:T(8,128)S(1)} %multiply_reduce_fusion.10, f32[4,8,128]{2,1,0:T(8,128)S(1)} %bitcast.58, f32[4,8,128]{2,1,0:T(8,128)S(1)} %get-tuple-element.649, f32[4,8,128]{2,1,0:T(8,128)S(1)} %bitcast.59, f32[4,128]{1,0:T(4,128)S(1)} %bitcast.66, ...), kind=kLoop, calls=%fused_computation.24.clone.1 | loop fusion | flops 9437184 | bytes 4265984 | tf_op jit(solution)/shard_map/while/body/mul | solution.py:99
  134.5 1.4 multiply_reduce_fusion.11
  137.1 1.3 multiply_reduce_fusion.10
  139.0 1.8 %fusion.20 = f32[4,8,128,128]{3,2,1,0:T(8,128)S(1)} fusion(f32[4,8,128,128]{3,2,1,0:T(8,128)S(1)} %multiply_reduce_fusion.10, f32[4,8,128]{2,1,0:T(8,128)S(1)} %bitcast.58, f32[4,8,128]{2,1,0:T(8,128)S(1)} %get-tuple-element.649, f32[4,8,128]{2,1,0:T(8,128)S(1)} %bitcast.59, f32[4,128]{1,0:T(4,128)S(1)} %bitcast.66, ...), kind=kLoop, calls=%fused_computation.24.clone.1 | loop fusion | flops 9437184 | bytes 4265984 | tf_op jit(solution)/shard_map/while/body/mul | solution.py:99
  140.8 1.4 multiply_reduce_fusion.11
  143.4 1.3 multiply_reduce_fusion.10
  145.3 1.8 %fusion.20 = f32[4,8,128,128]{3,2,1,0:T(8,128)S(1)} fusion(f32[4,8,128,128]{3,2,1,0:T(8,128)S(1)} %multiply_reduce_fusion.10, f32[4,8,128]{2,1,0:T(8,128)S(1)} %bitcast.58, f32[4,8,128]{2,1,0:T(8,128)S(1)} %get-tuple-element.649, f32[4,8,128]{2,1,0:T(8,128)S(1)} %bitcast.59, f32[4,128]{1,0:T(4,128)S(1)} %bitcast.66, ...), kind=kLoop, calls=%fused_computation.24.clone.1 | loop fusion | flops 9437184 | bytes 4265984 | tf_op jit(solution)/shard_map/while/body/mul | solution.py:99
  147.2 1.4 multiply_reduce_fusion.11
  149.7 1.3 multiply_reduce_fusion.10
  151.6 1.8 %fusion.20 = f32[4,8,128,128]{3,2,1,0:T(8,128)S(1)} fusion(f32[4,8,128,128]{3,2,1,0:T(8,128)S(1)} %multiply_reduce_fusion.10, f32[4,8,128]{2,1,0:T(8,128)S(1)} %bitcast.58, f32[4,8,128]{2,1,0:T(8,128)S(1)} %get-tuple-element.649, f32[4,8,128]{2,1,0:T(8,128)S(1)} %bitcast.59, f32[4,128]{1,0:T(4,128)S(1)} %bitcast.66, ...), kind=kLoop, calls=%fused_computation.24.clone.1 | loop fusion | flops 9437184 | bytes 4265984 | tf_op jit(solution)/shard_map/while/body/mul | solution.py:99
  153.5 1.4 multiply_reduce_fusion.11
  155.1 0.6 gather_fusion.1
  156.0 1.3 multiply_reduce_fusion.10
  157.9 1.8 %fusion.20 = f32[4,8,128,128]{3,2,1,0:T(8,128)S(1)} fusion(f32[4,8,128,128]{3,2,1,0:T(8,128)S(1)} %multiply_reduce_fusion.10, f32[4,8,128]{2,1,0:T(8,128)S(1)} %bitcast.58, f32[4,8,128]{2,1,0:T(8,128)S(1)} %get-tuple-element.649, f32[4,8,128]{2,1,0:T(8,128)S(1)} %bitcast.59, f32[4,128]{1,0:T(4,128)S(1)} %bitcast.66, ...), kind=kLoop, calls=%fused_computation.24.clone.1 | loop fusion | flops 9437184 | bytes 4265984 | tf_op jit(solution)/shard_map/while/body/mul | solution.py:99
  159.8 1.4 multiply_reduce_fusion.11
  161.4 0.6 gather_fusion.1
  162.4 1.3 multiply_reduce_fusion.10
  164.2 1.8 %fusion.20 = f32[4,8,128,128]{3,2,1,0:T(8,128)S(1)} fusion(f32[4,8,128,128]{3,2,1,0:T(8,128)S(1)} %multiply_reduce_fusion.10, f32[4,8,128]{2,1,0:T(8,128)S(1)} %bitcast.58, f32[4,8,128]{2,1,0:T(8,128)S(1)} %get-tuple-element.649, f32[4,8,128]{2,1,0:T(8,128)S(1)} %bitcast.59, f32[4,128]{1,0:T(4,128)S(1)} %bitcast.66, ...), kind=kLoop, calls=%fused_computation.24.clone.1 | loop fusion | flops 9437184 | bytes 4265984 | tf_op jit(solution)/shard_map/while/body/mul | solution.py:99
  166.1 1.4 multiply_reduce_fusion.11
  168.7 1.3 multiply_reduce_fusion.10
  170.5 1.8 %fusion.20 = f32[4,8,128,128]{3,2,1,0:T(8,128)S(1)} fusion(f32[4,8,128,128]{3,2,1,0:T(8,128)S(1)} %multiply_reduce_fusion.10, f32[4,8,128]{2,1,0:T(8,128)S(1)} %bitcast.58, f32[4,8,128]{2,1,0:T(8,128)S(1)} %get-tuple-element.649, f32[4,8,128]{2,1,0:T(8,128)S(1)} %bitcast.59, f32[4,128]{1,0:T(4,128)S(1)} %bitcast.66, ...), kind=kLoop, calls=%fused_computation.24.clone.1 | loop fusion | flops 9437184 | bytes 4265984 | tf_op jit(solution)/shard_map/while/body/mul | solution.py:99
  172.4 1.4 multiply_reduce_fusion.11
  173.8 0.6 copy.21
  (275 shorter events, 19.2 us)
Async XLA Ops:
  0.6 59.5 %copy-start.3 = (f32[3]{0:T(128)S(1)}, f32[3]{0:T(128)}, u32[]{:S(2)}) copy-start(f32[3]{0:T(128)} %constant.159.clone..sunk.6) | copy-start | bytes 40
  0.6 59.5 %copy-start.4 = (s32[4]{0:T(128)S(1)}, s32[4]{0:T(128)}, u32[]{:S(2)}) copy-start(s32[4]{0:T(128)} %param.12) | copy-start | bytes 52
  40.3 18.9 %collective-permute-start = (f32[128,5,128]{2,1,0:T(8,128)S(1)}, f32[128,5,128]{2,1,0:T(8,128)S(1)}, u32[]{:S(2)}, u32[]{:S(2)}) collective-permute-start(f32[128,5,128]{2,1,0:T(8,128)S(1)} %all_gather.3), channel_id=1, source_target_pairs={{0,32},{32,64},{64,96},{96,128},{128,160},{160,192},{192,224},{224... | collective-permute-start | bytes 983048 | tf_op jit(solution)/shard_map/ppermute | solution.py:20
  43.5 16.7 %collective-permute-start.1 = (f32[128,5,128]{2,1,0:T(8,128)S(1)}, f32[128,5,128]{2,1,0:T(8,128)S(1)}, u32[]{:S(2)}, u32[]{:S(2)}) collective-permute-start(f32[128,5,128]{2,1,0:T(8,128)S(1)} %all_gather.3), channel_id=1, source_target_pairs={{32,0},{64,32},{96,64},{128,96},{160,128},{192,160},{224,192},{256... | collective-permute-start | bytes 983048 | tf_op jit(solution)/shard_map/ppermute | solution.py:23
  60.2 31.6 %copy-start.5 = (f32[4,128]{1,0:T(4,128)S(1)}, f32[4,128]{1,0:T(4,128)}, u32[]{:S(2)}) copy-start(f32[4,128]{1,0:T(4,128)} %param.10) | copy-start | bytes 6148
  91.8 31.5 %copy-start.2 = (f32[4,128]{1,0:T(4,128)}, f32[4,128]{1,0:T(4,128)S(1)}, u32[]{:S(2)}) copy-start(f32[4,128]{1,0:T(4,128)S(1)} %get-tuple-element.453) | copy-start | bytes 6148
  111.6 10.3 %collective-permute-start.2 = (f32[128,128]{1,0:T(8,128)S(1)}, f32[128,128]{1,0:T(8,128)S(1)}, u32[]{:S(2)}, u32[]{:S(2)}) collective-permute-start(f32[128,128]{1,0:T(8,128)S(1)} %bitcast.62), channel_id=1, source_target_pairs={{0,32},{32,64},{64,96},{96,128},{128,160},{160,192},{192,224},{224... | collective-permute-start | bytes 196616 | tf_op jit(solution)/shard_map/ppermute | solution.py:20
  113.6 9.7 %collective-permute-start.3 = (f32[128,128]{1,0:T(8,128)S(1)}, f32[128,128]{1,0:T(8,128)S(1)}, u32[]{:S(2)}, u32[]{:S(2)}) collective-permute-start(f32[128,128]{1,0:T(8,128)S(1)} %bitcast.63), channel_id=1, source_target_pairs={{32,0},{64,32},{96,64},{128,96},{160,128},{192,160},{224,192},{256... | collective-permute-start | bytes 196616 | tf_op jit(solution)/shard_map/ppermute | solution.py:23
  123.3 1.2 copy-start
  128.2 1.4 copy-start.1
  129.7 1.2 copy-start
  134.5 1.4 copy-start.1
  136.0 1.2 copy-start
  140.8 1.4 copy-start.1
  142.3 1.2 copy-start
  147.1 1.4 copy-start.1
  148.6 1.2 copy-start
  153.4 1.4 copy-start.1
  154.9 1.2 copy-start
  159.8 1.4 copy-start.1
  161.2 1.2 copy-start
  166.1 1.4 copy-start.1
  167.5 1.2 copy-start
  172.4 1.4 copy-start.1
where the time goes:
time: 176 us; the launch traced here: 174 us
  other arithmetic  66.7 us (38%)
  blocking collectives  58.7 us (33%)
  local copies, waits for them, and re-layouts  19.5 us (11%)
  starting transfers between devices  19.1 us (11%)
  waiting for transfers between devices  7.49 us (4%)
    all_gather x1, blocking collectives, on_device(): gathered = lax.all_gather(particles, 'dev', axis=0, tiled=True)  39 us
    reduce_sum x16, other arithmetic, fetch_block(): dist_sq = jnp.sum(offset * offset, axis=2)  20.8 us
    all_to_all x1, blocking collectives, copy_for_each(): return lax.all_to_all(copies, axis, split_axis=0, concat_axis=0, tiled=True)  19.8 us
    mul x8, other arithmetic, force_step(): live[:, :, None, None] * others[:, :, 3, None, :]  14.7 us
    ppermute x2, starting transfers between devices, padded(): lax.ppermute(lax.slice_in_dim(block, 0, width, axis=dim), axis, backward)  14.1 us
    reduce_sum x8, other arithmetic, density_step(): jnp.sum(live[:, :, None, None] * others[:, :, 3, None, :] * kernel, axis=...  11.6 us
    reduce_sum x8, other arithmetic, force_step(): return total - jnp.sum(factor[:, :, None] * offset, axis=(1, 4))  11 us
    gather x16, local copies, waits for them, and re-layouts, fetch_block(): others = extended[chosen]  9.36 us
  transfers between devices with their start and end apart: 4, of which 3 were waited for; matrix products, arithmetic and copies ran while one was open for 2% of the time, Pallas kernels for 0%

commit v1 on v0

v1 whole, which is shorter than its diff:
```python
import math

import jax
import jax.numpy as jnp
from jax import lax
from jax.experimental import pallas as pl
from jax.experimental.pallas import tpu as pltpu
from jax.sharding import PartitionSpec as P

MESH = pl.DeviceIdType.MESH
GROUPS = 16
ROWS = 16
CORES = 2
OWN = 4
LANES = 128
SLOTS = 64
GROUP_CELLS = ROWS * CORES * OWN
GROUP_BITS = 7
BLOCKS = 3 * CORES * ROWS
CELLS = BLOCKS * OWN
FEAT = 16
NORM = 21.0 / (16.0 * math.pi)
TINY = 1e-12


def block_at(region, core, row):
    return (region * ROWS + row) * CORES + core


def high(values):
    return values.astype(jnp.bfloat16).astype(jnp.float32)


def kernel(
    lists, counts, part, entropy, dens_out, acc_out,
    ext, hext, wext, feat, mom, left, invh, dist, cube, first,
    zsend, zrecv, fsend, frecv,
):
    grp = lax.axis_index("grp")
    dev = lax.axis_index("dev")
    row = dev // CORES
    core = dev % CORES
    mate = row * CORES + (1 - core)
    above = lax.rem(grp + 1, GROUPS)
    below = lax.rem(grp + GROUPS - 1, GROUPS)
    mine = block_at(1, core, row)
    targets = ((above, dev, 0), (below, dev, 2), (above, mate, 0), (below, mate, 2), (grp, mate, 1))

    def column(step):
        return lax.rem(row + step, ROWS) * CORES + core

    barrier = pltpu.get_barrier_semaphore()
    far_first = (8, 7, 9, 6, 10, 5, 11, 4, 12, 3, 13, 2, 14, 1, 15)
    for step in far_first:
        pl.semaphore_signal(barrier, inc=1, device_id=(grp, column(step)), device_id_type=MESH)
    for group, member, _ in targets:
        pl.semaphore_signal(barrier, inc=1, device_id=(group, member), device_id_type=MESH)

    rows_mine = pl.multiple_of(mine * OWN * 4, 16)
    for cell in range(OWN):
        ext[pl.ds(rows_mine + 4 * cell, 4), :] = part[cell, 0:4, :]
        hext[mine, cell : cell + 1, :] = part[cell, 4:5, :]

    def ext_block(at, count=1):
        return ext.at[pl.ds(pl.multiple_of(at * OWN * 4, 16), count * OWN * 4)]

    def h_block(at, count=1):
        return hext.at[pl.ds(at, count)]

    def w_block(at, count=1):
        return wext.at[pl.ds(at, count)]

    def send_column(which, block):
        for step in far_first:
            pltpu.make_async_remote_copy(
                src_ref=block(mine),
                dst_ref=block(mine),
                send_sem=zsend.at[which],
                recv_sem=zrecv.at[which, row],
                device_id=(grp, column(step)),
                device_id_type=MESH,
            ).start()

    def forward(which, block, at_row):
        at = block_at(1, core, at_row)
        for number, (group, member, region) in enumerate(targets):
            pltpu.make_async_remote_copy(
                src_ref=block(at),
                dst_ref=block(block_at(region, core, at_row)),
                send_sem=fsend.at[which, number],
                recv_sem=frecv.at[which, region],
                device_id=(group, member),
                device_id_type=MESH,
            ).start()

    def wait_for(ref, sem):
        pltpu.make_async_copy(ref, ref, sem).wait()

    def forward_rest(which, block):
        def step(number, carry):
            half = (number + 1) // 2
            at_row = lax.rem(row + ROWS + lax.rem(number, 2) * 2 * half - half, ROWS)
            wait_for(block(block_at(1, core, at_row)), zrecv.at[which, at_row])
            forward(which, block, at_row)
            return carry

        lax.fori_loop(1, ROWS, step, 0)

    def arrived(which, block):
        wait_for(block(block_at(1, 0, 0), ROWS), frecv.at[which, 1])
        wait_for(block(block_at(0, 0, 0), 2 * ROWS), frecv.at[which, 0])
        wait_for(block(block_at(2, 0, 0), 2 * ROWS), frecv.at[which, 2])

    def all_sent(which, block):
        wait_for(block(0, ROWS - 1), zsend.at[which])
        for number in range(len(targets)):
            wait_for(block(0, ROWS), fsend.at[which, number])

    pl.semaphore_wait(barrier, len(far_first) + len(targets))
    send_column(0, ext_block)
    forward(0, ext_block, row)
    send_column(1, h_block)
    forward(1, h_block, row)

    zero_row = jnp.zeros((1, LANES), jnp.float32)
    one_row = jnp.ones((1, LANES), jnp.float32)
    for cell in range(OWN):
        coords = [part[cell, axis : axis + 1, :] - 0.5 for axis in range(3)]
        highs = [high(value) for value in coords]
        lows = [high(value - top) for value, top in zip(coords, highs)]
        square = zero_row
        for top, low in zip(highs, lows):
            square = square + (top + low) * (top + low)
        part_a = high(square)
        part_b = high(square - part_a)
        part_c = square - part_a - part_b
        minus_high = [-2.0 * value for value in highs]
        minus_low = [-2.0 * value for value in lows]
        stacked = jnp.concatenate(
            minus_high + minus_high + [one_row] * 3 + [part_a, part_b, part_c] + [zero_row] * 4
            + minus_low + minus_low + [zero_row] * 10,
            axis=0,
        )
        wide = jnp.concatenate([stacked, jnp.zeros((LANES - 2 * FEAT, LANES), jnp.float32)], axis=0)
        left[cell] = wide.T[:, : 2 * FEAT].astype(jnp.bfloat16)
        invh[cell] = jnp.broadcast_to(2.0 / part[cell, 4:5, :], (LANES, LANES)).T

    def slot_cell(cell, number):
        ident = lists[cell, number]
        region = (lax.shift_right_logical(ident, GROUP_BITS) - grp + (GROUPS + 1)) & (GROUPS - 1)
        at = region * GROUP_CELLS + (ident & (GROUP_CELLS - 1))
        live = jnp.minimum(jnp.maximum(counts[cell] - number, 0), 1)
        return CELLS + live * (at - CELLS)

    feat[pl.ds(CELLS * FEAT, FEAT), :] = jnp.zeros((FEAT, LANES), jnp.float32)
    mom[pl.ds(CELLS * 8, 8), :] = jnp.zeros((8, LANES), jnp.float32)
    wext[BLOCKS] = jnp.zeros((OWN, LANES), jnp.float32)
    ones = jnp.ones((8, LANES), jnp.float32)
    zeros = jnp.zeros((8, LANES), jnp.float32)

    forward_rest(0, ext_block)
    forward_rest(1, h_block)
    arrived(0, ext_block)

    def features(number, carry):
        region = number // ROWS
        middle = 0.5 - (region - 1).astype(jnp.float32)

        def plane(axis):
            return ext[pl.ds(number * 32 + axis, 8, stride=4), :]

        coords = [plane(0) - middle, plane(1) - 0.5, plane(2) - 0.5]
        mass = plane(3)
        highs = [high(value) for value in coords]
        lows = [high(value - top) for value, top in zip(coords, highs)]
        square = zeros
        for top, low in zip(highs, lows):
            square = square + (top + low) * (top + low)
        part_a = high(square)
        part_b = high(square - part_a)
        part_c = square - part_a - part_b
        planes = highs + lows + [part_a, part_b, part_c, ones, ones, ones, mass, zeros, zeros, zeros]
        for at, value in enumerate(planes):
            feat[pl.ds(number * 8 * FEAT + at, 8, stride=FEAT), :] = value
        moments = [mass] + [mass * value for value in coords]
        for at, value in enumerate(moments + moments):
            mom[pl.ds(number * 64 + at, 8, stride=8), :] = value
        return carry

    lax.fori_loop(0, CELLS // 8, features, 0)

    def feature_rows(at):
        return feat[pl.ds(at * FEAT, FEAT), :]

    def density_cell(cell, carry):
        lhs = left[cell]
        scale = invh[cell]

        def step(pair, total):
            ids = [slot_cell(cell, 2 * pair + which) for which in range(2)]
            rows = [feature_rows(at) for at in ids]
            rhs = jnp.concatenate(rows, axis=1).astype(jnp.bfloat16)
            rhs = jnp.concatenate([rhs, rhs], axis=0)
            square = jnp.dot(lhs, rhs, preferred_element_type=jnp.float32)
            for which in range(2):
                part_sq = jnp.maximum(square[:, which * LANES : (which + 1) * LANES], TINY)
                gap = part_sq * lax.rsqrt(part_sq)
                dist[cell * SLOTS + 2 * pair + which] = gap
                base = jnp.maximum(4.0 - gap * scale, 0.0)
                base_sq = base * base
                total = total + base_sq * base_sq * (5.0 - base) * rows[which][12:13, :]
            return total

        total = lax.fori_loop(0, SLOTS // 2, step, jnp.zeros((LANES, LANES), jnp.float32))
        summed = jnp.sum(total.T, axis=0, keepdims=True)
        smooth = part[cell, 4:5, :]
        density = summed * (NORM / 256.0) / (smooth * smooth * smooth)
        weight = entropy[pl.ds(cell, 1), :] * jnp.exp(jnp.log(density) * (-1.0 / 3.0))
        dens_out[pl.ds(cell, 1), :] = density
        wext[mine, pl.ds(cell, 1), :] = weight
        return carry

    lax.fori_loop(0, OWN, density_cell, 0)

    send_column(2, w_block)
    forward(2, w_block, row)

    arrived(1, h_block)

    def smoothing(number, carry):
        smooth = jnp.concatenate([hext[2 * number], hext[2 * number + 1]], axis=0)
        inverse = 1.0 / smooth
        square = inverse * inverse
        feat[pl.ds(number * 8 * FEAT + 13, 8, stride=FEAT), :] = 2.0 * inverse
        feat[pl.ds(number * 8 * FEAT + 14, 8, stride=FEAT), :] = square * square * inverse
        return carry

    lax.fori_loop(0, CELLS // 8, smoothing, 0)

    upper = lax.broadcasted_iota(jnp.int32, (8, 2 * LANES), 0) < 4

    def split(values):
        top = high(values)
        return jnp.where(upper, top, values - top).astype(jnp.bfloat16)

    def moment_rows(at):
        return mom[pl.ds(at * 8, 8), :]

    across = (((1,), (1,)), ((), ()))

    def first_cell(cell, carry):
        scale = invh[cell]

        def step(pair, total):
            ids = [slot_cell(cell, 2 * pair + which) for which in range(2)]
            moments = jnp.concatenate([moment_rows(at) for at in ids], axis=1)
            cubes = []
            for which in range(2):
                gap = dist[cell * SLOTS + 2 * pair + which]
                base = jnp.maximum(4.0 - gap * scale, 0.0)
                cubes.append((base * base * base).astype(jnp.bfloat16))
                other = jnp.maximum(4.0 - gap * feature_rows(ids[which])[13:14, :], 0.0)
                cube[cell * SLOTS + 2 * pair + which] = (other * other * other).astype(jnp.bfloat16)
            return total + lax.dot_general(
                split(moments), jnp.concatenate(cubes, axis=1), across, preferred_element_type=jnp.float32
            )

        first[cell] = lax.fori_loop(0, SLOTS // 2, step, jnp.zeros((8, LANES), jnp.float32))
        return carry

    lax.fori_loop(0, OWN, first_cell, 0)
    forward_rest(2, w_block)
    arrived(2, w_block)

    def force_cell(cell, carry):
        def step(pair, total):
            ids = [slot_cell(cell, 2 * pair + which) for which in range(2)]
            scaled = []
            for at in ids:
                factor = wext[lax.shift_right_logical(at, 2), pl.ds(at & 3, 1), :] * feature_rows(at)[14:15, :]
                scaled.append(moment_rows(at) * factor)
            cubes = [cube[cell * SLOTS + 2 * pair + which] for which in range(2)]
            return total + lax.dot_general(
                split(jnp.concatenate(scaled, axis=1)),
                jnp.concatenate(cubes, axis=1),
                across,
                preferred_element_type=jnp.float32,
            )

        second = lax.fori_loop(0, SLOTS // 2, step, jnp.zeros((8, LANES), jnp.float32))
        second = second[0:4] + second[4:8]
        ahead = first[cell]
        ahead = ahead[0:4] + ahead[4:8]
        inverse = 1.0 / part[cell, 4:5, :]
        square = inverse * inverse
        own = wext[mine, pl.ds(cell, 1), :] * (square * square * inverse)
        joint = (own * ahead + second) * (5.0 * NORM / 64.0)
        coords = part[cell, 0:3, :] - 0.5
        acc_out[cell] = coords * joint[0:1] - joint[1:4]
        return carry

    lax.fori_loop(0, OWN, force_cell, 0)
    all_sent(0, ext_block)
    all_sent(1, h_block)
    all_sent(2, w_block)


def on_device(particles, entropy, lists, counts):
    vmem = pl.BlockSpec(memory_space=pltpu.VMEM)
    smem = pl.BlockSpec(memory_space=pltpu.SMEM)
    f32, bf16 = jnp.float32, jnp.bfloat16
    return pl.pallas_call(
        kernel,
        out_shape=(
            jax.ShapeDtypeStruct((OWN, LANES), f32),
            jax.ShapeDtypeStruct((OWN, 3, LANES), f32),
        ),
        in_specs=[smem, smem, vmem, vmem],
        out_specs=(vmem, vmem),
        scratch_shapes=[
            pltpu.VMEM((CELLS * 4, LANES), f32),
            pltpu.VMEM((BLOCKS, OWN, LANES), f32),
            pltpu.VMEM((BLOCKS + 1, OWN, LANES), f32),
            pltpu.VMEM(((CELLS + 1) * FEAT, LANES), f32),
            pltpu.VMEM(((CELLS + 1) * 8, LANES), f32),
            pltpu.VMEM((OWN, LANES, 2 * FEAT), bf16),
            pltpu.VMEM((OWN, LANES, LANES), f32),
            pltpu.VMEM((OWN * SLOTS, LANES, LANES), f32),
            pltpu.VMEM((OWN * SLOTS, LANES, LANES), bf16),
            pltpu.VMEM((OWN, 8, LANES), f32),
            pltpu.SemaphoreType.DMA((3,)),
            pltpu.SemaphoreType.DMA((3, ROWS)),
            pltpu.SemaphoreType.DMA((3, 5)),
            pltpu.SemaphoreType.DMA((3, 3)),
        ],
        compiler_params=pltpu.CompilerParams(
            collective_id=0, has_side_effects=True, vmem_limit_bytes=48 * 1024 * 1024
        ),
        name="sph",
    )(lists, counts, particles, entropy)


def solution(mesh):
    return jax.shard_map(
        on_device,
        mesh=mesh,
        in_specs=(
            P(("grp", "dev"), None, None),
            P(("grp", "dev"), None),
            P(("grp", "dev"), None),
            P(("grp", "dev")),
        ),
        out_specs=(P(("grp", "dev"), None), P(("grp", "dev"), None, None)),
        check_vma=False,
    )
```

time: 176 us -> 109 us (0.62)
  Pallas kernels: 0 us -> 106 us
  other arithmetic: 66.7 us -> 0 us
  blocking collectives: 58.7 us -> 0 us
  starting transfers between devices: 19.1 us -> 0 us
  local copies, waits for them, and re-layouts: 19.5 us -> 1.91 us
  waiting for transfers between devices: 7.49 us -> 0 us
    pallas_call x0 -> x1, Pallas kernels: none -> 106 us  [on_device(): pl.pallas_call(kernel, out_shape=(jax.ShapeDtypeStruct((OWN, LANES), f32)...]
    reduce_sum x32 -> x0, other arithmetic: 43.4 us -> none  [the longest x16 20.8 us: fetch_block(): dist_sq = jnp.sum(offset * offset, axis=2)]
    all_gather x1 -> x0, blocking collectives: 39 us -> none  [on_device(): gathered = lax.all_gather(particles, 'dev', axis=0, tiled=True)]
    all_to_all x1 -> x0, blocking collectives: 19.8 us -> none  [copy_for_each(): return lax.all_to_all(copies, axis, split_axis=0, concat_axis=0, tiled=True)]
    ppermute x4 -> x0, starting transfers between devices: 19.1 us -> none  [the longest x2 14.1 us: padded(): lax.ppermute(lax.slice_in_dim(block, 0, width, axis=dim), axis, backward)]
    mul x41 -> x0, other arithmetic: 17.7 us -> none  [the longest x8 14.7 us: force_step(): live[:, :, None, None] * others[:, :, 3, None, :]]
    gather x24 -> x0, local copies, waits for them, and re-layouts: 14 us -> none  [the longest x16 9.36 us: fetch_block(): others = extended[chosen]]
    ppermute x4 -> x0, waiting for transfers between devices: 7.49 us -> none  [the longest x2 5.41 us: padded(): lax.ppermute(lax.slice_in_dim(block, block.shape[dim] - width, None, axis...]
  transfers between devices with their start and end apart: 4 -> 0, of which waited for: 3 -> 0; matrix products, arithmetic and copies ran while one was open for 2% -> 0% of each run, Pallas kernels for 0% -> 0%
where the time goes in v1:
time: 109 us
  Pallas kernels  106 us (97%)
  local copies, waits for them, and re-layouts  1.91 us (2%)
    pallas_call x1, Pallas kernels, on_device(): pl.pallas_call(kernel, out_shape=(jax.ShapeDtypeStruct((OWN, LANES), f32)...  106 us

profile of v1, /device:TPU:1, one launch (start us, length us, event | category | flops | bytes accessed | tf_op | source)
XLA Modules:
  0.0 109.1 jit_solution(60755232495835572)
XLA Ops:
  0.6 0.0 copy-start.2
  0.6 0.0 copy-start
  0.7 0.0 copy-start.1
  0.7 0.7 copy.6.part
  1.4 0.0 copy-done.2
  1.4 0.0 copy-done
  1.4 0.0 copy-done.1
  1.4 106.5 %sph.1 = (f32[4,128]{1,0:T(4,128)S(1)}, f32[4,3,128]{2,1,0:T(4,128)S(1)}) custom-call(s32[4,64]{1,0:T(4,128)S(1)} %copy-done, s32[4]{0:T(128)S(1)} %copy-done.2, f32[4,5,128]{2,1,0:T(8,128)S(1)} %copy.6.part, f32[4,128]{1,0:T(4,128)S(1)} %copy-done.1), custom_call_target="tpu_custom_call" | custom-call | tf_op jit(solution)/shard_map/sph/pallas_call | solution.py:312
  107.9 0.6 copy.7
  108.5 0.6 copy.9
Async XLA Ops:
  0.6 0.8 copy-start.2
  0.6 0.7 copy-start
  0.7 0.7 copy-start.1

commit v2 on v1

--- a/solution.py
+++ b/solution.py
@@ -21,6 +21,9 @@
 FEAT = 16
 NORM = 21.0 / (16.0 * math.pi)
 TINY = 1e-12
+DENSITY_PAIRS = 8
+FIRST_SLOTS = 16
+FORCE_SLOTS = 32
 
 
 def block_at(region, core, row):
@@ -196,22 +199,23 @@
         lhs = left[cell]
         scale = invh[cell]
 
-        def step(pair, total):
-            ids = [slot_cell(cell, 2 * pair + which) for which in range(2)]
-            rows = [feature_rows(at) for at in ids]
-            rhs = jnp.concatenate(rows, axis=1).astype(jnp.bfloat16)
-            rhs = jnp.concatenate([rhs, rhs], axis=0)
-            square = jnp.dot(lhs, rhs, preferred_element_type=jnp.float32)
-            for which in range(2):
-                part_sq = jnp.maximum(square[:, which * LANES : (which + 1) * LANES], TINY)
-                gap = part_sq * lax.rsqrt(part_sq)
-                dist[cell * SLOTS + 2 * pair + which] = gap
-                base = jnp.maximum(4.0 - gap * scale, 0.0)
-                base_sq = base * base
-                total = total + base_sq * base_sq * (5.0 - base) * rows[which][12:13, :]
+        def step(turn, total):
+            for pair in range(DENSITY_PAIRS):
+                slot = (turn * DENSITY_PAIRS + pair) * 2
+                rows = [feature_rows(slot_cell(cell, slot + which)) for which in range(2)]
+                rhs = jnp.concatenate(rows, axis=1).astype(jnp.bfloat16)
+                rhs = jnp.concatenate([rhs, rhs], axis=0)
+                square = jnp.dot(lhs, rhs, preferred_element_type=jnp.float32)
+                for which in range(2):
+                    part_sq = jnp.maximum(square[:, which * LANES : (which + 1) * LANES], TINY)
+                    gap = part_sq * lax.rsqrt(part_sq)
+                    dist[cell * SLOTS + slot + which] = gap
+                    base = jnp.maximum(4.0 - gap * scale, 0.0)
+                    base_sq = base * base
+                    total = total + base_sq * base_sq * (5.0 - base) * rows[which][12:13, :]
             return total
 
-        total = lax.fori_loop(0, SLOTS // 2, step, jnp.zeros((LANES, LANES), jnp.float32))
+        total = lax.fori_loop(0, SLOTS // (2 * DENSITY_PAIRS), step, jnp.zeros((LANES, LANES), jnp.float32))
         summed = jnp.sum(total.T, axis=0, keepdims=True)
         smooth = part[cell, 4:5, :]
         density = summed * (NORM / 256.0) / (smooth * smooth * smooth)
@@ -237,7 +241,7 @@
 
     lax.fori_loop(0, CELLS // 8, smoothing, 0)
 
-    upper = lax.broadcasted_iota(jnp.int32, (8, 2 * LANES), 0) < 4
+    upper = lax.broadcasted_iota(jnp.int32, (8, LANES), 0) < 4
 
     def split(values):
         top = high(values)
@@ -251,21 +255,23 @@
     def first_cell(cell, carry):
         scale = invh[cell]
 
-        def step(pair, total):
-            ids = [slot_cell(cell, 2 * pair + which) for which in range(2)]
-            moments = jnp.concatenate([moment_rows(at) for at in ids], axis=1)
-            cubes = []
-            for which in range(2):
-                gap = dist[cell * SLOTS + 2 * pair + which]
+        def step(turn, total):
+            tops, cubes = [], []
+            for each in range(FIRST_SLOTS):
+                slot = turn * FIRST_SLOTS + each
+                at = slot_cell(cell, slot)
+                tops.append(split(moment_rows(at)))
+                gap = dist[cell * SLOTS + slot]
                 base = jnp.maximum(4.0 - gap * scale, 0.0)
                 cubes.append((base * base * base).astype(jnp.bfloat16))
-                other = jnp.maximum(4.0 - gap * feature_rows(ids[which])[13:14, :], 0.0)
-                cube[cell * SLOTS + 2 * pair + which] = (other * other * other).astype(jnp.bfloat16)
+                other = jnp.maximum(4.0 - gap * feature_rows(at)[13:14, :], 0.0)
+                cube[cell * SLOTS + slot] = (other * other * other).astype(jnp.bfloat16)
             return total + lax.dot_general(
-                split(moments), jnp.concatenate(cubes, axis=1), across, preferred_element_type=jnp.float32
+                jnp.concatenate(tops, axis=1), jnp.concatenate(cubes, axis=1), across,
+                preferred_element_type=jnp.float32,
             )
 
-        first[cell] = lax.fori_loop(0, SLOTS // 2, step, jnp.zeros((8, LANES), jnp.float32))
+        first[cell] = lax.fori_loop(0, SLOTS // FIRST_SLOTS, step, jnp.zeros((8, LANES), jnp.float32))
         return carry
 
     lax.fori_loop(0, OWN, first_cell, 0)
@@ -273,21 +279,20 @@
     arrived(2, w_block)
 
     def force_cell(cell, carry):
-        def step(pair, total):
-            ids = [slot_cell(cell, 2 * pair + which) for which in range(2)]
-            scaled = []
-            for at in ids:
+        def step(turn, total):
+            tops, cubes = [], []
+            for each in range(FORCE_SLOTS):
+                slot = turn * FORCE_SLOTS + each
+                at = slot_cell(cell, slot)
                 factor = wext[lax.shift_right_logical(at, 2), pl.ds(at & 3, 1), :] * feature_rows(at)[14:15, :]
-                scaled.append(moment_rows(at) * factor)
-            cubes = [cube[cell * SLOTS + 2 * pair + which] for which in range(2)]
+                tops.append(split(moment_rows(at) * factor))
+                cubes.append(cube[cell * SLOTS + slot])
             return total + lax.dot_general(
-                split(jnp.concatenate(scaled, axis=1)),
-                jnp.concatenate(cubes, axis=1),
-                across,
+                jnp.concatenate(tops, axis=1), jnp.concatenate(cubes, axis=1), across,
                 preferred_element_type=jnp.float32,
             )
 
-        second = lax.fori_loop(0, SLOTS // 2, step, jnp.zeros((8, LANES), jnp.float32))
+        second = lax.fori_loop(0, SLOTS // FORCE_SLOTS, step, jnp.zeros((8, LANES), jnp.float32))
         second = second[0:4] + second[4:8]
         ahead = first[cell]
         ahead = ahead[0:4] + ahead[4:8]

time: 109 us -> 64.9 us (0.60)
  Pallas kernels: 106 us -> 62.2 us
    pallas_call x1, Pallas kernels: 106 us -> 62.2 us  [on_device(): pl.pallas_call(kernel, out_shape=(jax.ShapeDtypeStruct((OWN, LANES), f32)...]
where the time goes in v2:
time: 64.9 us; the launch traced here: 64.7 us
  Pallas kernels  62.2 us (96%)
  local copies, waits for them, and re-layouts  1.91 us (3%)
  between operations  0.67 us (1%)
    pallas_call x1, Pallas kernels, on_device(): pl.pallas_call(kernel, out_shape=(jax.ShapeDtypeStruct((OWN, LANES), f32)...  62.2 us
    unnamed x8, local copies, waits for them, and re-layouts  1.31 us

profile of v2, /device:TPU:1, one launch (start us, length us, event | category | flops | bytes accessed | tf_op | source)
XLA Modules:
  0.0 64.7 jit_solution(8173203768400169416)
XLA Ops:
  0.6 0.0 copy-start.2
  0.6 0.0 copy-start
  0.7 0.0 copy-start.1
  0.7 0.7 %copy.6.part = f32[4,5,128]{2,1,0:T(8,128)S(1)} copy(f32[4,5,128]{2,0,1:T(4,128)} %param.4) | data formatting | bytes 20480 | tf_op args[0]
  1.4 0.0 copy-done.2
  1.4 0.0 copy-done
  1.4 0.0 copy-done.1
  1.4 62.2 %sph.1 = (f32[4,128]{1,0:T(4,128)S(1)}, f32[4,3,128]{2,1,0:T(4,128)S(1)}) custom-call(s32[4,64]{1,0:T(4,128)S(1)} %copy-done, s32[4]{0:T(128)S(1)} %copy-done.2, f32[4,5,128]{2,1,0:T(8,128)S(1)} %copy.6.part, f32[4,128]{1,0:T(4,128)S(1)} %copy-done.1), custom_call_target="tpu_custom_call" | custom-call | tf_op jit(solution)/shard_map/sph/pallas_call | solution.py:317
  63.6 0.6 copy.7
  64.2 0.6 copy.9
Async XLA Ops:
  0.6 0.8 %copy-start.2 = (s32[4]{0:T(128)S(1)}, s32[4]{0:T(128)}, u32[]{:S(2)}) copy-start(s32[4]{0:T(128)} %counts.1) | copy-start | bytes 52
  0.6 0.7 %copy-start = (s32[4,64]{1,0:T(4,128)S(1)}, s32[4,64]{1,0:T(4,128)}, u32[]{:S(2)}) copy-start(s32[4,64]{1,0:T(4,128)} %lists.1) | copy-start | bytes 3076
  0.7 0.7 %copy-start.1 = (f32[4,128]{1,0:T(4,128)S(1)}, f32[4,128]{1,0:T(4,128)}, u32[]{:S(2)}) copy-start(f32[4,128]{1,0:T(4,128)} %entropy.1) | copy-start | bytes 6148

commit v3 on v2

--- a/solution.py
+++ b/solution.py
@@ -21,13 +21,13 @@
 FEAT = 16
 NORM = 21.0 / (16.0 * math.pi)
 TINY = 1e-12
-DENSITY_PAIRS = 8
+DENSITY_PAIRS = 16
 FIRST_SLOTS = 16
-FORCE_SLOTS = 32
+FORCE_SLOTS = 64
 
 
 def block_at(region, core, row):
-    return (region * ROWS + row) * CORES + core
+    return (region * CORES + core) * ROWS + row
 
 
 def high(values):
@@ -53,8 +53,9 @@
         return lax.rem(row + step, ROWS) * CORES + core
 
     barrier = pltpu.get_barrier_semaphore()
-    far_first = (8, 7, 9, 6, 10, 5, 11, 4, 12, 3, 13, 2, 14, 1, 15)
-    for step in far_first:
+    near = (1, 15, 2, 14, 3, 13, 4, 12)
+    far = (8, 7, 9, 6, 10, 5, 11)
+    for step in near:
         pl.semaphore_signal(barrier, inc=1, device_id=(grp, column(step)), device_id_type=MESH)
     for group, member, _ in targets:
         pl.semaphore_signal(barrier, inc=1, device_id=(group, member), device_id_type=MESH)
@@ -73,23 +74,23 @@
     def w_block(at, count=1):
         return wext.at[pl.ds(at, count)]
 
-    def send_column(which, block):
-        for step in far_first:
-            pltpu.make_async_remote_copy(
-                src_ref=block(mine),
-                dst_ref=block(mine),
-                send_sem=zsend.at[which],
-                recv_sem=zrecv.at[which, row],
-                device_id=(grp, column(step)),
-                device_id_type=MESH,
-            ).start()
-
-    def forward(which, block, at_row):
+    def send_row(which, block, at_row, step):
+        at = block_at(1, core, at_row)
+        pltpu.make_async_remote_copy(
+            src_ref=block(at),
+            dst_ref=block(at),
+            send_sem=zsend.at[which],
+            recv_sem=zrecv.at[which, at_row],
+            device_id=(grp, column(step)),
+            device_id_type=MESH,
+        ).start()
+
+    def forward(which, block, at_row, count):
         at = block_at(1, core, at_row)
         for number, (group, member, region) in enumerate(targets):
             pltpu.make_async_remote_copy(
-                src_ref=block(at),
-                dst_ref=block(block_at(region, core, at_row)),
+                src_ref=block(at, count),
+                dst_ref=block(block_at(region, core, at_row), count),
                 send_sem=fsend.at[which, number],
                 recv_sem=frecv.at[which, region],
                 device_id=(group, member),
@@ -99,15 +100,44 @@
     def wait_for(ref, sem):
         pltpu.make_async_copy(ref, ref, sem).wait()
 
-    def forward_rest(which, block):
-        def step(number, carry):
-            half = (number + 1) // 2
-            at_row = lax.rem(row + ROWS + lax.rem(number, 2) * 2 * half - half, ROWS)
-            wait_for(block(block_at(1, core, at_row)), zrecv.at[which, at_row])
-            forward(which, block, at_row)
+    def landed(which, block, at_row):
+        wait_for(block(block_at(1, core, at_row)), zrecv.at[which, at_row])
+
+    def row_at(number):
+        half = (number + 1) // 2
+        return lax.rem(row + ROWS + lax.rem(number, 2) * 2 * half - half, ROWS)
+
+    def pass_on(which, block):
+        forward(which, block, row, 1)
+
+        def close(number, carry):
+            at_row = row_at(number)
+            landed(which, block, at_row)
+            send_row(which, block, at_row, ROWS + 4 - 8 * lax.rem(number, 2))
+            forward(which, block, at_row, 1)
             return carry
 
-        lax.fori_loop(1, ROWS, step, 0)
+        def rest(number, carry):
+            at_row = row_at(number)
+            landed(which, block, at_row)
+            forward(which, block, at_row, 1)
+            return carry
+
+        lax.fori_loop(1, 7, close, 0)
+        rest(jnp.int32(7), 0)
+        at_row = lax.rem(row + ROWS - 4, ROWS)
+        landed(which, block, at_row)
+        send_row(which, block, at_row, 4)
+        forward(which, block, at_row, 1)
+        lax.fori_loop(9, ROWS, rest, 0)
+
+    def pass_whole(which, block):
+        def one(number, carry):
+            landed(which, block, lax.rem(row + number, ROWS))
+            return carry
+
+        lax.fori_loop(1, ROWS, one, 0)
+        forward(which, block, 0, ROWS)
 
     def arrived(which, block):
         wait_for(block(block_at(1, 0, 0), ROWS), frecv.at[which, 1])
@@ -119,11 +149,11 @@
         for number in range(len(targets)):
             wait_for(block(0, ROWS), fsend.at[which, number])
 
-    pl.semaphore_wait(barrier, len(far_first) + len(targets))
-    send_column(0, ext_block)
-    forward(0, ext_block, row)
-    send_column(1, h_block)
-    forward(1, h_block, row)
+    pl.semaphore_wait(barrier, len(near) + len(targets))
+    for step in near:
+        send_row(0, ext_block, row, step)
+    for step in near:
+        send_row(1, h_block, row, step)
 
     zero_row = jnp.zeros((1, LANES), jnp.float32)
     one_row = jnp.ones((1, LANES), jnp.float32)
@@ -151,7 +181,8 @@
     def slot_cell(cell, number):
         ident = lists[cell, number]
         region = (lax.shift_right_logical(ident, GROUP_BITS) - grp + (GROUPS + 1)) & (GROUPS - 1)
-        at = region * GROUP_CELLS + (ident & (GROUP_CELLS - 1))
+        plane = lax.shift_left(ident & OWN, 4)
+        at = region * GROUP_CELLS + plane + (lax.shift_right_logical(ident, 1) & 60) + (ident & (OWN - 1))
         live = jnp.minimum(jnp.maximum(counts[cell] - number, 0), 1)
         return CELLS + live * (at - CELLS)
 
@@ -161,19 +192,31 @@
     ones = jnp.ones((8, LANES), jnp.float32)
     zeros = jnp.zeros((8, LANES), jnp.float32)
 
-    forward_rest(0, ext_block)
-    forward_rest(1, h_block)
+    def settle(number, carry):
+        rows = number * 8 * FEAT
+        for at in (9, 10, 11):
+            feat[pl.ds(rows + at, 8, stride=FEAT), :] = ones
+        for at in (13, 14, 15):
+            feat[pl.ds(rows + at, 8, stride=FEAT), :] = zeros
+        return carry
+
+    lax.fori_loop(0, CELLS // 8, settle, 0)
+    pass_on(0, ext_block)
+    for step in far:
+        send_row(1, h_block, row, step)
     arrived(0, ext_block)
 
-    def features(number, carry):
+    def planes(number):
         region = number // ROWS
         middle = 0.5 - (region - 1).astype(jnp.float32)
 
         def plane(axis):
             return ext[pl.ds(number * 32 + axis, 8, stride=4), :]
 
-        coords = [plane(0) - middle, plane(1) - 0.5, plane(2) - 0.5]
-        mass = plane(3)
+        return [plane(0) - middle, plane(1) - 0.5, plane(2) - 0.5], plane(3)
+
+    def features(number, carry):
+        coords, mass = planes(number)
         highs = [high(value) for value in coords]
         lows = [high(value - top) for value, top in zip(coords, highs)]
         square = zeros
@@ -182,12 +225,9 @@
         part_a = high(square)
         part_b = high(square - part_a)
         part_c = square - part_a - part_b
-        planes = highs + lows + [part_a, part_b, part_c, ones, ones, ones, mass, zeros, zeros, zeros]
-        for at, value in enumerate(planes):
+        for at, value in enumerate(highs + lows + [part_a, part_b, part_c]):
             feat[pl.ds(number * 8 * FEAT + at, 8, stride=FEAT), :] = value
-        moments = [mass] + [mass * value for value in coords]
-        for at, value in enumerate(moments + moments):
-            mom[pl.ds(number * 64 + at, 8, stride=8), :] = value
+        feat[pl.ds(number * 8 * FEAT + 12, 8, stride=FEAT), :] = mass
         return carry
 
     lax.fori_loop(0, CELLS // 8, features, 0)
@@ -226,10 +266,19 @@
 
     lax.fori_loop(0, OWN, density_cell, 0)
 
-    send_column(2, w_block)
-    forward(2, w_block, row)
-
-    arrived(1, h_block)
+    for step in far + near:
+        send_row(2, w_block, row, step)
+
+    pass_whole(1, h_block)
+
+    def moments(number, carry):
+        coords, mass = planes(number)
+        values = [mass] + [mass * value for value in coords]
+        for at, value in enumerate(values + values):
+            mom[pl.ds(number * 64 + at, 8, stride=8), :] = value
+        return carry
+
+    lax.fori_loop(0, CELLS // 8, moments, 0)
 
     def smoothing(number, carry):
         smooth = jnp.concatenate([hext[2 * number], hext[2 * number + 1]], axis=0)
@@ -239,7 +288,6 @@
         feat[pl.ds(number * 8 * FEAT + 14, 8, stride=FEAT), :] = square * square * inverse
         return carry
 
-    lax.fori_loop(0, CELLS // 8, smoothing, 0)
 
     upper = lax.broadcasted_iota(jnp.int32, (8, LANES), 0) < 4
 
@@ -264,8 +312,6 @@
                 gap = dist[cell * SLOTS + slot]
                 base = jnp.maximum(4.0 - gap * scale, 0.0)
                 cubes.append((base * base * base).astype(jnp.bfloat16))
-                other = jnp.maximum(4.0 - gap * feature_rows(at)[13:14, :], 0.0)
-                cube[cell * SLOTS + slot] = (other * other * other).astype(jnp.bfloat16)
             return total + lax.dot_general(
                 jnp.concatenate(tops, axis=1), jnp.concatenate(cubes, axis=1), across,
                 preferred_element_type=jnp.float32,
@@ -275,7 +321,23 @@
         return carry
 
     lax.fori_loop(0, OWN, first_cell, 0)
-    forward_rest(2, w_block)
+    arrived(1, h_block)
+    lax.fori_loop(0, CELLS // 8, smoothing, 0)
+
+    def cube_cell(cell, carry):
+        def step(turn, inner):
+            for each in range(FIRST_SLOTS):
+                slot = turn * FIRST_SLOTS + each
+                scale = feature_rows(slot_cell(cell, slot))[13:14, :]
+                other = jnp.maximum(4.0 - dist[cell * SLOTS + slot] * scale, 0.0)
+                cube[cell * SLOTS + slot] = (other * other * other).astype(jnp.bfloat16)
+            return inner
+
+        return lax.fori_loop(0, SLOTS // FIRST_SLOTS, step, carry)
+
+    lax.fori_loop(0, OWN - 2, cube_cell, 0)
+    pass_whole(2, w_block)
+    lax.fori_loop(OWN - 2, OWN, cube_cell, 0)
     arrived(2, w_block)
 
     def force_cell(cell, carry):

time: 64.9 us -> 60.9 us (0.938)
  Pallas kernels: 62.2 us -> 58.1 us
    pallas_call x1, Pallas kernels: 62.2 us -> 58.1 us  [on_device(): pl.pallas_call(kernel, out_shape=(jax.ShapeDtypeStruct((OWN, LANES), f32)...]
where the time goes in v3:
time: 60.9 us; the launch traced here: 60.7 us
  Pallas kernels  58.1 us (95%)
  local copies, waits for them, and re-layouts  1.91 us (3%)
  between operations  0.67 us (1%)
    pallas_call x1, Pallas kernels, on_device(): pl.pallas_call(kernel, out_shape=(jax.ShapeDtypeStruct((OWN, LANES), f32)...  58.1 us
    unnamed x8, local copies, waits for them, and re-layouts  1.31 us

profile of v3, /device:TPU:1, one launch (start us, length us, event | category | flops | bytes accessed | tf_op | source)
XLA Modules:
  0.0 60.7 jit_solution(9132602900028534866)
XLA Ops:
  0.6 0.0 copy-start.2
  0.6 0.0 copy-start
  0.7 0.0 copy-start.1
  0.7 0.7 %copy.6.part = f32[4,5,128]{2,1,0:T(8,128)S(1)} copy(f32[4,5,128]{2,0,1:T(4,128)} %param.4) | data formatting | bytes 20480 | tf_op args[0]
  1.4 0.0 copy-done.2
  1.4 0.0 copy-done
  1.4 0.0 copy-done.1
  1.4 58.1 %sph.1 = (f32[4,128]{1,0:T(4,128)S(1)}, f32[4,3,128]{2,1,0:T(4,128)S(1)}) custom-call(s32[4,64]{1,0:T(4,128)S(1)} %copy-done, s32[4]{0:T(128)S(1)} %copy-done.2, f32[4,5,128]{2,1,0:T(8,128)S(1)} %copy.6.part, f32[4,128]{1,0:T(4,128)S(1)} %copy-done.1), custom_call_target="tpu_custom_call" | custom-call | tf_op jit(solution)/shard_map/sph/pallas_call | solution.py:379
  59.5 0.6 copy.7
  60.1 0.6 copy.9
Async XLA Ops:
  0.6 0.8 %copy-start.2 = (s32[4]{0:T(128)S(1)}, s32[4]{0:T(128)}, u32[]{:S(2)}) copy-start(s32[4]{0:T(128)} %counts.1) | copy-start | bytes 52
  0.6 0.7 %copy-start = (s32[4,64]{1,0:T(4,128)S(1)}, s32[4,64]{1,0:T(4,128)}, u32[]{:S(2)}) copy-start(s32[4,64]{1,0:T(4,128)} %lists.1) | copy-start | bytes 3076
  0.7 0.7 %copy-start.1 = (f32[4,128]{1,0:T(4,128)S(1)}, f32[4,128]{1,0:T(4,128)}, u32[]{:S(2)}) copy-start(f32[4,128]{1,0:T(4,128)} %entropy.1) | copy-start | bytes 6148

commit v4 on v3

--- a/solution.py
+++ b/solution.py
@@ -21,7 +21,7 @@
 FEAT = 16
 NORM = 21.0 / (16.0 * math.pi)
 TINY = 1e-12
-DENSITY_PAIRS = 16
+DENSITY_PAIRS = 32
 FIRST_SLOTS = 16
 FORCE_SLOTS = 64
 
@@ -335,9 +335,9 @@
 
         return lax.fori_loop(0, SLOTS // FIRST_SLOTS, step, carry)
 
-    lax.fori_loop(0, OWN - 2, cube_cell, 0)
+    lax.fori_loop(0, OWN - 3, cube_cell, 0)
     pass_whole(2, w_block)
-    lax.fori_loop(OWN - 2, OWN, cube_cell, 0)
+    lax.fori_loop(OWN - 3, OWN, cube_cell, 0)
     arrived(2, w_block)
 
     def force_cell(cell, carry):

time: 60.9 us -> 59.4 us (0.975)
  Pallas kernels: 58.1 us -> 56.7 us
    pallas_call x1, Pallas kernels: 58.1 us -> 56.7 us  [on_device(): pl.pallas_call(kernel, out_shape=(jax.ShapeDtypeStruct((OWN, LANES), f32)...]
where the time goes in v4:
time: 59.4 us; the launch traced here: 59.3 us
  Pallas kernels  56.7 us (95%)
  local copies, waits for them, and re-layouts  1.91 us (3%)
  between operations  0.67 us (1%)
    pallas_call x1, Pallas kernels, on_device(): pl.pallas_call(kernel, out_shape=(jax.ShapeDtypeStruct((OWN, LANES), f32)...  56.7 us
    unnamed x8, local copies, waits for them, and re-layouts  1.31 us

profile of v4, /device:TPU:1, one launch (start us, length us, event | category | flops | bytes accessed | tf_op | source)
XLA Modules:
  0.0 59.3 jit_solution(10240989613823570120)
XLA Ops:
  0.6 0.0 copy-start.2
  0.6 0.0 copy-start
  0.7 0.0 copy-start.1
  0.7 0.7 %copy.6.part = f32[4,5,128]{2,1,0:T(8,128)S(1)} copy(f32[4,5,128]{2,0,1:T(4,128)} %param.4) | data formatting | bytes 20480 | tf_op args[0]
  1.4 0.0 copy-done.2
  1.4 0.0 copy-done
  1.4 0.0 copy-done.1
  1.4 56.7 %sph.1 = (f32[4,128]{1,0:T(4,128)S(1)}, f32[4,3,128]{2,1,0:T(4,128)S(1)}) custom-call(s32[4,64]{1,0:T(4,128)S(1)} %copy-done, s32[4]{0:T(128)S(1)} %copy-done.2, f32[4,5,128]{2,1,0:T(8,128)S(1)} %copy.6.part, f32[4,128]{1,0:T(4,128)S(1)} %copy-done.1), custom_call_target="tpu_custom_call" | custom-call | tf_op jit(solution)/shard_map/sph/pallas_call | solution.py:379
  58.1 0.6 %copy.7 = f32[4,3,128]{2,0,1:T(4,128)} copy(f32[4,3,128]{2,1,0:T(4,128)S(1)} %get-tuple-element.3) | data formatting | bytes 12288 | tf_op jit(solution)/shard_map/sph/pallas_call | solution.py:379
  58.7 0.6 copy.9
Async XLA Ops:
  0.6 0.8 %copy-start.2 = (s32[4]{0:T(128)S(1)}, s32[4]{0:T(128)}, u32[]{:S(2)}) copy-start(s32[4]{0:T(128)} %counts.1) | copy-start | bytes 52
  0.6 0.7 %copy-start = (s32[4,64]{1,0:T(4,128)S(1)}, s32[4,64]{1,0:T(4,128)}, u32[]{:S(2)}) copy-start(s32[4,64]{1,0:T(4,128)} %lists.1) | copy-start | bytes 3076
  0.7 0.7 %copy-start.1 = (f32[4,128]{1,0:T(4,128)S(1)}, f32[4,128]{1,0:T(4,128)}, u32[]{:S(2)}) copy-start(f32[4,128]{1,0:T(4,128)} %entropy.1) | copy-start | bytes 6148
